TPU v7x, 128 devices: a whole 4x4x4 slice. The times are simulated.
128 devices in a mesh: visit: 4 (over x), patch: 32 (over z, y, core).
Axes of the slice: x: 4, y: 4, z: 4, core: 2. Of those that a mesh axis runs over, the one named last changes fastest.
Arguments:
- warp_image: float32 [3072, 84, 512], P(('visit', 'patch')), may hold values from -6 to 6
- warp_variance: float32 [3072, 64, 512], P(('visit', 'patch')), may hold values from 0.25 to 4
- kernel_coef: float32 [3072, 40], P(('visit', 'patch')), may hold values from -0.6 to 0.6
- tile_patch: int32 [3072, 1], P(('visit', 'patch')), may hold values from 0 to 31; in each aligned block of 24 rows (0 to 23, 24 to 47, ...) at most 2 rows name the same one
Outputs:
- coadd: float32 [32, 64, 512], P('patch', 'visit')
Inputs may be any that keep to these rules, and one draw needn't show every extreme that they name: `tile_patch`: in the rows of one device no patch is named by more than 2 tiles, and every patch is named by some tile.
All inputs are finite; a program needn't handle non-finite values.
Results may differ from a plain program's by a relative error of at most 0.0057.
Values may be sent and summed in bfloat16 or wider, within the bound.
A program may use at most 128 MiB of HBM per device.

v0:
```python
import jax
import jax.numpy as jnp
from jax import lax
from jax.sharding import PartitionSpec as P

KHALF = 10


def basis_table():
    offsets = jnp.arange(2 * KHALF + 1, dtype=jnp.float32) - float(KHALF)
    scaled = offsets / float(KHALF)
    basis_terms = []
    for spread_px, degree in ((1.0, 4), (2.5, 4), (5.0, 3)):
        profile = jnp.exp(-offsets * offsets / (2.0 * spread_px * spread_px))
        for power_a in range(degree + 1):
            for power_b in range(degree + 1 - power_a):
                basis_terms.append(jnp.outer(profile * scaled**power_a, profile * scaled**power_b))
    return jnp.stack(basis_terms)


def band_table():
    taps = 2 * KHALF + 1
    window_pos = jnp.arange(256, dtype=jnp.int32)[:, None]
    out_pos = jnp.arange(128, dtype=jnp.int32)[None, :]
    differ = window_pos - out_pos
    tap_ids = jnp.arange(taps, dtype=jnp.int32)[:, None, None]
    return (differ[None] == tap_ids).astype(jnp.bfloat16)


def match_tile(tile_image, kernel_taps, band_set):
    rows = tile_image.shape[0] - 2 * KHALF
    columns = tile_image.shape[1]
    toeplitz = jnp.einsum(
        "us,swk->uwk", kernel_taps, band_set, preferred_element_type=jnp.float32
    ).astype(jnp.bfloat16)
    padded = jnp.pad(tile_image, ((0, 0), (KHALF, 128 - KHALF)))
    windows = jnp.stack(
        [
            padded[:, 128 * block_index : 128 * block_index + 256]
            for block_index in range(columns // 128)
        ],
        axis=1,
    )
    shifted = jnp.stack([windows[offset : offset + rows] for offset in range(2 * KHALF + 1)])
    result = jnp.einsum("urjw,uwk->rjk", shifted, toeplitz, preferred_element_type=jnp.float32)
    return result.reshape(rows, columns).astype(jnp.bfloat16)


def on_device(warp_image, warp_variance, kernel_coef, tile_patch):
    tile_count = warp_image.shape[0]
    rows = warp_variance.shape[1]
    columns = warp_variance.shape[2]
    patch_count = lax.axis_size("patch")
    capacity = max(2, 3 * tile_count // patch_count)
    slot_count = patch_count * capacity
    basis_set = basis_table()
    band_set = band_table()
    kernels = jnp.einsum("tb,buv->tuv", kernel_coef, basis_set, precision=lax.Precision.HIGHEST)
    kernel_power = jnp.mean(kernels * kernels, axis=(1, 2)) + 1e-06
    weight = (1.0 / (warp_variance * kernel_power[:, None, None])).astype(jnp.bfloat16)
    kernel_taps = kernels.astype(jnp.bfloat16)
    targets = tile_patch[:, 0]
    same_patch = (targets[:, None] == targets[None, :]).astype(jnp.int32)
    row_ids = jnp.arange(tile_count, dtype=jnp.int32)
    earlier = (row_ids[:, None] > row_ids[None, :]).astype(jnp.int32)
    slot_rank = jnp.sum(same_patch * earlier, axis=1)
    slot_index = targets * capacity + slot_rank
    weight_slots = jnp.zeros((slot_count, rows, columns), jnp.bfloat16).at[slot_index].set(weight)
    image_slots = (
        jnp.zeros((slot_count,) + warp_image.shape[1:], jnp.bfloat16)
        .at[slot_index]
        .set(warp_image.astype(jnp.bfloat16))
    )
    kernel_slots = (
        jnp.zeros((slot_count,) + kernel_taps.shape[1:], jnp.bfloat16)
        .at[slot_index]
        .set(kernel_taps)
    )
    got_image, got_weight, got_kernel = (
        lax.all_to_all(image_slots, "patch", split_axis=0, concat_axis=0, tiled=True),
        lax.all_to_all(weight_slots, "patch", split_axis=0, concat_axis=0, tiled=True),
        lax.all_to_all(kernel_slots, "patch", split_axis=0, concat_axis=0, tiled=True),
    )

    def match_slot(operands):
        slot_image, slot_kernel, slot_weight = operands
        return lax.cond(
            jnp.max(slot_weight.astype(jnp.float32)) > 0.0,
            lambda: match_tile(slot_image, slot_kernel, band_set),
            lambda: jnp.zeros((rows, columns), jnp.bfloat16),
        )

    matched = lax.map(match_slot, (got_image, got_kernel, got_weight))
    weight_full = got_weight.astype(jnp.float32)
    numerator = jnp.sum(weight_full * matched.astype(jnp.float32), axis=0)
    denominator = jnp.sum(weight_full, axis=0)
    numerator, denominator = lax.psum((numerator, denominator), "visit")
    share_rows = rows // lax.axis_size("visit")
    first_row = lax.axis_index("visit") * share_rows
    numerator = lax.dynamic_slice_in_dim(numerator, first_row, share_rows, 0)
    denominator = lax.dynamic_slice_in_dim(denominator, first_row, share_rows, 0)
    return (numerator / denominator)[None]


def solution(mesh):
    return jax.shard_map(
        on_device,
        mesh=mesh,
        in_specs=(
            P(("visit", "patch"), None, None),
            P(("visit", "patch"), None, None),
            P(("visit", "patch"), None),
            P(("visit", "patch"), None),
        ),
        out_specs=P("patch", "visit", None),
        check_vma=False,
    )
```

profile of v0, /device:TPU:1, one launch (start us, length us, event | category | flops | bytes accessed | tf_op | source)
XLA Modules:
  0.0 649.9 jit_solution(4562838191714787050)
XLA Ops:
  13.3 9.6 %all-to-all-start.2 = ((bf16[32,2,441]{2,1,0:T(2,128)(2,1)}), bf16[32,2,441]{2,1,0:T(2,128)(2,1)S(1)}, u32[]{:S(2)}, u32[]{:S(2)}) async-start(bf16[32,2,441]{2,1,0:T(2,128)(2,1)} %reshape.1883), calls=%async_computation.2 | async-start | bytes 131072 | tf_op jit(solution)/shard_map/all_to_all | solution.py:82
  27.8 5.4 scatter_fusion
  33.2 7.4 %all-to-all-start = ((bf16[64,64,512]{2,1,0:T(8,128)(2,1)}), bf16[64,64,512]{2,1,0:T(8,128)(2,1)}, u32[]{:S(2)}, u32[]{:S(2)}) async-start(bf16[64,64,512]{2,1,0:T(8,128)(2,1)} %scatter_fusion), calls=%async_computation | async-start | bytes 8388608 | tf_op jit(solution)/shard_map/all_to_all | solution.py:81
  46.6 7.0 %scatter_fusion.1 = bf16[64,84,512]{2,1,0:T(8,128)(2,1)} fusion(bf16[64,84,512]{2,1,0:T(8,128)(2,1)} %broadcast_in_dim.13, s32[24]{0:T(128)S(1)} %fusion.41, bf16[24,84,512]{2,1,0:T(8,128)(2,1)S(1)} %copy.122), kind=kCustom, calls=%fused_computation.1 | custom fusion | bytes 6193248 | tf_op jit(solution)/shard_map/scatter | solution.py:72
  53.6 37.2 %all-to-all-done = bf16[64,64,512]{2,1,0:T(8,128)(2,1)} async-done(((bf16[64,64,512]{2,1,0:T(8,128)(2,1)}), bf16[64,64,512]{2,1,0:T(8,128)(2,1)}, u32[]{:S(2)}, u32[]{:S(2)}) %all-to-all-start) | async-done | bytes 4194336 | tf_op jit(solution)/shard_map/all_to_all | solution.py:81
  90.8 8.0 %all-to-all-start.1 = ((bf16[64,84,512]{2,1,0:T(8,128)(2,1)}), bf16[64,84,512]{2,1,0:T(8,128)(2,1)}, u32[]{:S(2)}, u32[]{:S(2)}) async-start(bf16[64,84,512]{2,1,0:T(8,128)(2,1)} %scatter_fusion.1), calls=%async_computation.1 | async-start | bytes 11534336 | tf_op jit(solution)/shard_map/all_to_all | solution.py:80
  99.4 66.6 %all-to-all-done.1 = bf16[64,84,512]{2,1,0:T(8,128)(2,1)} async-done(((bf16[64,84,512]{2,1,0:T(8,128)(2,1)}), bf16[64,84,512]{2,1,0:T(8,128)(2,1)}, u32[]{:S(2)}, u32[]{:S(2)}) %all-to-all-start.1) | async-done | bytes 5505056 | tf_op jit(solution)/shard_map/all_to_all | solution.py:80
  168.5 276.6 %while.13 = (s32[]{:T(128)}, bf16[64,64,512]{2,1,0:T(8,128)(2,1)}, bf16[64,64,512]{2,1,0:T(8,128)(2,1)}, bf16[64,84,512]{2,1,0:T(8,128)(2,1)}, bf16[64,21,21]{2,...) while((s32[]{:T(128)}, bf16[64,64,512]{2,1,0:T(8,128)(2,1)}, ...), condition=%wide.region_9.10_spmd.clone, body=%wide.region_5.9_spmd.clone.sunk | while | flops 383610880 | bytes 15489687 | solution.py:93
  171.1 3.5 conditional.3
  181.1 3.5 conditional.3
  197.5 3.5 conditional.3
  220.4 3.5 conditional.3
  250.2 3.5 conditional.3
  260.1 3.5 conditional.3
  289.5 3.5 conditional.3
  299.5 3.5 conditional.3
  309.4 3.5 conditional.3
  319.4 3.5 conditional.3
  339.2 3.5 conditional.3
  378.6 3.5 conditional.3
  395.0 3.5 conditional.3
  421.4 3.5 conditional.3
  445.1 5.8 fusion.38
  451.0 190.7 %all-reduce.4.cloned.1.call-done = (f32[64,512]{1,0:T(8,128)}, f32[64,512]{1,0:T(8,128)}) async-done(((f32[64,512]{1,0:T(8,128)}, f32[64,512]{1,0:T(8,128)}), (f32[64,512]{1,0:T(8,128)}, f32[64,512]{1,0:T(8,128)})) %all-reduce.4.cloned.1.call-update) | async-done | bytes 262160 | tf_op jit(solution)/shard_map/psum | solution.py:97
  (880 shorter events, 271.3 us)
Async XLA Ops:
  6.5 2.9 copy-start
  13.3 19.9 %all-to-all-start.2 = ((bf16[32,2,441]{2,1,0:T(2,128)(2,1)}), bf16[32,2,441]{2,1,0:T(2,128)(2,1)S(1)}, u32[]{:S(2)}, u32[]{:S(2)}) async-start(bf16[32,2,441]{2,1,0:T(2,128)(2,1)} %reshape.1883), calls=%async_computation.2 | async-start | bytes 131072 | tf_op jit(solution)/shard_map/all_to_all | solution.py:82
  33.2 57.6 %all-to-all-start = ((bf16[64,64,512]{2,1,0:T(8,128)(2,1)}), bf16[64,64,512]{2,1,0:T(8,128)(2,1)}, u32[]{:S(2)}, u32[]{:S(2)}) async-start(bf16[64,64,512]{2,1,0:T(8,128)(2,1)} %scatter_fusion), calls=%async_computation | async-start | bytes 8388608 | tf_op jit(solution)/shard_map/all_to_all | solution.py:81
  90.8 75.2 %all-to-all-start.1 = ((bf16[64,84,512]{2,1,0:T(8,128)(2,1)}), bf16[64,84,512]{2,1,0:T(8,128)(2,1)}, u32[]{:S(2)}, u32[]{:S(2)}) async-start(bf16[64,84,512]{2,1,0:T(8,128)(2,1)} %scatter_fusion.1), calls=%async_computation.1 | async-start | bytes 11534336 | tf_op jit(solution)/shard_map/all_to_all | solution.py:80
  98.8 542.9 %all-reduce.4.cloned.1.call-start = ((), (), s32[]{:S(2)}) async-start(), calls=%async_computation.3 | async-start | bytes 524288 | tf_op jit(solution)/shard_map/psum | solution.py:97
Sparse Core Ops, SparseCore 0:
  451.1 190.5 all-reduce.3
where the time goes:
time: 658 us; the launch traced here: 650 us
  waiting for transfers between devices  295 us (45%)
  other arithmetic  136 us (21%)
  local copies, waits for them, and re-layouts  101 us (15%)
  loops' own time  49.5 us (8%)
  matrix products  30.1 us (5%)
  starting transfers between devices  25.2 us (4%)
  between operations  13.6 us (2%)
    psum x1, waiting for transfers between devices, on_device(): numerator, denominator = lax.psum((numerator, denominator), 'visit')  191 us
    reduce_max x64, other arithmetic, match_slot(): jnp.max(slot_weight.astype(jnp.float32)) > 0.0  98.9 us
    all_to_all x1, waiting for transfers between devices, on_device(): lax.all_to_all(image_slots, 'patch', split_axis=0, concat_axis=0, tiled=T...  66.6 us
    another operation x1, loops' own time, on_device(): matched = lax.map(match_slot, (got_image, got_kernel, got_weight))  44.3 us
    dynamic_update_slice x64, local copies, waits for them, and re-layouts, on_device(): matched = lax.map(match_slot, (got_image, got_kernel, got_weight))  40.2 us
    all_to_all x1, waiting for transfers between devices, on_device(): lax.all_to_all(weight_slots, 'patch', split_axis=0, concat_axis=0, tiled=...  37.2 us
    convert_element_type x64, other arithmetic, band_table(): return (differ[None] == tap_ids).astype(jnp.bfloat16)  22.4 us
    squeeze x20, local copies, waits for them, and re-layouts, on_device(): matched = lax.map(match_slot, (got_image, got_kernel, got_weight))  18.1 us
  transfers between devices with their start and end apart: 4, of which 3 were waited for; matrix products, arithmetic and copies ran while one was open for 4% of the time, Pallas kernels for 0%

commit v1 on v0

v1 whole, which is shorter than its diff:
```python
import functools

import jax
import jax.numpy as jnp
import numpy as np
from jax import lax
from jax.experimental import pallas as pl
from jax.experimental.pallas import tpu as pltpu
from jax.sharding import PartitionSpec as P

KHALF = 10
TAPS = 2 * KHALF + 1
T = 24
ROWS = 64
COLS = 512
NPATCH = 32
BLK = 88
NK = 14
KDIM = 1280
NC = 2
W = COLS // NC
CB = W // 128
UNITS = 2 * CB
G = 2
NG = T // G
HI = lax.Precision.HIGHEST
F32 = jnp.float32
BF16 = jnp.bfloat16
MESH = pl.DeviceIdType.MESH


def tables():
    offsets = np.arange(TAPS, dtype=np.float64) - KHALF
    scaled = offsets / KHALF
    functions, place, terms = [], {}, []
    levels = ((1.0, 4), (2.5, 4), (5.0, 3))
    for s, (spread, degree) in enumerate(levels):
        profile = np.exp(-offsets * offsets / (2.0 * spread * spread))
        for i in range(degree + 1):
            place[s, i] = len(functions)
            functions.append(profile * scaled**i)
    for s, (spread, degree) in enumerate(levels):
        for i in range(degree + 1):
            for j in range(degree + 1 - i):
                terms.append((place[s, i], place[s, j]))
    g = np.array(functions)
    basis = np.zeros((len(terms), 512))
    for b, (ia, jb) in enumerate(terms):
        basis[b, : TAPS * TAPS] = np.outer(g[ia], g[jb]).reshape(-1)
    q = np.linalg.qr(g.T)[0]
    q = q.astype(jnp.bfloat16).astype(np.float64)
    mix = np.linalg.lstsq(q, g.T, rcond=None)[0]
    horizontal = np.zeros((256, NK * 128))
    for k in range(NK):
        for c in range(128):
            horizontal[c : c + TAPS, k * 128 + c] = q[:, k]
    vertical = np.zeros((len(terms), KDIM))
    for b, (ia, jb) in enumerate(terms):
        for k in range(NK):
            vertical[b, k * BLK : k * BLK + TAPS] = g[ia] * mix[k, jb]
    return basis.astype(np.float32), horizontal.astype(jnp.bfloat16), vertical.astype(np.float32)


def prepare_tile(t, x_ref, p_ref, v_ref, v0_ref):
    x = jnp.concatenate([x_ref.at[j][pl.ds(t, 84, stride=T), :] for j in range(4)], axis=1)
    x = jnp.concatenate([x, jnp.zeros((BLK - 84, COLS), F32)], axis=0)
    x = jnp.concatenate([x, jnp.zeros((BLK, 128), F32)], axis=1)
    x = pltpu.roll(x, KHALF, 1)
    p = jnp.concatenate([x[:, 128 * j : 128 * j + 256] for j in range(4)], axis=0)
    p_ref[t] = p.astype(BF16)
    row = jnp.broadcast_to(v0_ref[pl.ds(t, 1), :], (ROWS, KDIM))
    v_ref[t] = pltpu.roll(row, 0, 1, stride=1, stride_axis=0).astype(BF16)


def filter_columns(first, ch, p_ref, h_ref, y_ref):
    rows = BLK * CB
    lhs = jnp.concatenate([p_ref[first + u, rows * ch : rows * ch + rows, :] for u in range(G)], axis=0)
    for m in range(NK // 2):
        r = jnp.dot(lhs, h_ref[:, 256 * m : 256 * m + 256], preferred_element_type=F32)
        for u in range(G):
            for b in range(CB):
                o = rows * u + BLK * b
                y = jnp.concatenate([r[o : o + BLK, :128], r[o : o + BLK, 128:]], axis=0)
                y_ref[u, 2 * BLK * m : 2 * BLK * m + 2 * BLK, 128 * b : 128 * b + 128] = y.astype(BF16)


def match_rows(first, ch, v_ref, y_ref, var_ref, kp_ref, sum_ref):
    for u in range(G):
        t = first + u
        matched = jnp.dot(v_ref[t], y_ref[u], preferred_element_type=F32)
        w = (1.0 / (var_ref[t, :, W * ch : W * ch + W] * kp_ref[t])).astype(BF16).astype(F32)
        sum_ref[0, t] = w * matched
        sum_ref[1, t] = w


def place_coefs(a):
    cx = jnp.where(a == 0, 16, jnp.where(a == 1, 1, 4))
    cy = jnp.where(a == 0, 4, jnp.where(a == 1, 16, 1))
    cz = jnp.where(a == 0, 1, jnp.where(a == 1, 4, 16))
    return cx, cy, cz


def kernel(
    x_hbm, var_hbm, c_ref, tp_ref, bp_ref, h_ref, a_ref, out_ref,
    x_ref, var_ref, p_ref, v_ref, v0_ref, ya, yb, kp_ref, sum_ref,
    iv_ref, idx_ref, d_ref, own_ref, rc_ref, r1_ref, s1_ref, r2_ref, s2_ref, r3_ref, fin_ref,
    sx, sv, si, cs, cr, s1s, s1r, s2s, s2r, s3s, s3r,
):
    me_x = lax.axis_index("visit")
    me_p = lax.axis_index("patch")
    core = lax.rem(me_p, 2)
    me_y = lax.rem(me_p // 2, 4)
    me_z = me_p // 8

    def device(x, y, z, k):
        return (x, z * 8 + y * 2 + k)

    sibling = device(me_x, me_y, me_z, 1 - core)

    cpx = [
        pltpu.make_async_copy(
            x_hbm.at[pl.ds(T * 14 * (i // 4), T * 14), pl.ds(128 * (i % 4), 128)],
            x_ref.at[i % 4, pl.ds(T * 14 * (i // 4), T * 14)], sx.at[i])
        for i in range(24)
    ]
    cpv = [pltpu.make_async_copy(var_hbm.at[t], var_ref.at[t], sv.at[t]) for t in range(T)]
    for cp in cpx + cpv:
        cp.start()

    barrier = pltpu.get_barrier_semaphore()
    pl.semaphore_signal(barrier, inc=1, device_id=sibling, device_id_type=MESH)
    for d in range(1, 4):
        for who in (
            device(lax.rem(me_x + d, 4), me_y, me_z, core),
            device(me_x, lax.rem(me_y + d, 4), me_z, core),
            device(me_x, me_y, lax.rem(me_z + d, 4), core),
        ):
            pl.semaphore_signal(barrier, inc=1, device_id=who, device_id_type=MESH)

    lane = lax.broadcasted_iota(jnp.int32, (8, 128), 1)
    one = jnp.full((8, 128), T, jnp.int32)
    two = one
    for t in range(T):
        hit = lane == tp_ref[0, t]
        two = jnp.where(hit, one, two)
        one = jnp.where(hit, t, one)
    iv_ref[0:8, :] = one
    iv_ref[8:16, :] = two
    cpi = pltpu.make_async_copy(iv_ref, idx_ref, si)
    cpi.start()

    c = c_ref[...]
    taps = jnp.dot(c, bp_ref[...], precision=HI, preferred_element_type=F32)
    kp = jnp.sum(taps * taps, axis=1, keepdims=True) / float(TAPS * TAPS) + 1e-6
    for t in range(T):
        kp_ref[t] = jnp.broadcast_to(kp[t : t + 1], (1, W))
    v0_ref[...] = jnp.dot(c, a_ref[...], precision=HI, preferred_element_type=F32)
    for y in (ya, yb):
        for u in range(G):
            y[u, NK * BLK :, :] = jnp.zeros((KDIM - NK * BLK, W), BF16)
    for nd in range(2):
        sum_ref[nd, T] = jnp.zeros((ROWS, W), F32)
    for cp in cpx:
        cp.wait()

    def prepare(t, carry):
        prepare_tile(t, x_ref, p_ref, v_ref, v0_ref)
        return carry

    lax.fori_loop(0, T, prepare, 0)
    for cp in cpv:
        cp.wait()
    cpi.wait()

    def axis_of(u, k):
        return lax.rem(u + k, 3)

    def along(a, step, d):
        b = lax.rem(a + step, 3)
        here = jnp.where(b == 0, me_x, jnp.where(b == 1, me_y, me_z))
        there = lax.rem(here + d, 4)
        who = device(
            jnp.where(b == 0, there, me_x), jnp.where(b == 1, there, me_y), jnp.where(b == 2, there, me_z), core)
        return here, there, who

    def gather(k, store):
        def body(i, carry):
            z, y = i // 4, lax.rem(i, 4)
            p = z * 8 + y * 2 + k
            i1, i2 = idx_ref[0, p], idx_ref[8, p]
            for nd in range(2):
                s = sum_ref[nd, i1] + sum_ref[nd, i2]
                for cb in range(CB):
                    u = nd * CB + cb
                    cx, cy, cz = place_coefs(axis_of(u, k))
                    for x in range(4):
                        store(u, cx * x + cy * y + cz * z, s[16 * x : 16 * x + 16, 128 * cb : 128 * cb + 128])
            return carry
        lax.fori_loop(0, 16, body, 0)

    def core_copy(ch, u):
        return pltpu.make_async_remote_copy(
            src_ref=d_ref.at[ch, u], dst_ref=rc_ref.at[ch, u], send_sem=cs.at[ch, u], recv_sem=cr.at[ch, u],
            device_id=sibling, device_id_type=MESH)

    def copy1(ch, u, d):
        here, there, who = along(axis_of(u, core), 0, d)
        return pltpu.make_async_remote_copy(
            src_ref=rc_ref.at[ch, u, pl.ds(there * 16, 16)], dst_ref=r1_ref.at[ch, u, d - 1],
            send_sem=s1s.at[ch, u, d - 1], recv_sem=s1r.at[ch, u, d - 1], device_id=who, device_id_type=MESH)

    def copy2(ch, u, d):
        here, there, who = along(axis_of(u, core), 1, d)
        return pltpu.make_async_remote_copy(
            src_ref=s1_ref.at[ch, u, pl.ds(there * 4, 4)], dst_ref=r2_ref.at[ch, u, d - 1],
            send_sem=s2s.at[ch, u, d - 1], recv_sem=s2r.at[ch, u, d - 1], device_id=who, device_id_type=MESH)

    def copy3(ch, u, d):
        here, there, who = along(axis_of(u, core), 2, d)
        return pltpu.make_async_remote_copy(
            src_ref=s2_ref.at[ch, u, there], dst_ref=r3_ref.at[ch, u, d - 1],
            send_sem=s3s.at[ch, u, d - 1], recv_sem=s3r.at[ch, u, d - 1], device_id=who, device_id_type=MESH)

    def start_core(ch):
        def put(u, place, value):
            d_ref[ch, u, place] = value.astype(BF16)
        gather(1 - core, put)
        for u in range(UNITS):
            core_copy(ch, u).start()

        def keep(u, place, value):
            own_ref[u, place] = value
        gather(core, keep)

    def start_1(ch):
        for u in range(UNITS):
            core_copy(ch, u).wait_recv()

            def body(i, carry):
                at = pl.ds(i * 8, 8)
                rc_ref[ch, u, at] = (rc_ref[ch, u, at].astype(F32) + own_ref[u, at]).astype(BF16)
                return carry
            lax.fori_loop(0, 8, body, 0)
            for d in (2, 1, 3):
                copy1(ch, u, d).start()

    def start_2(ch):
        for u in range(UNITS):
            for d in range(1, 4):
                copy1(ch, u, d).wait_recv()
            here = along(axis_of(u, core), 0, 0)[0]
            total = rc_ref[ch, u, pl.ds(here * 16, 16)].astype(F32)
            for d in range(3):
                total = total + r1_ref[ch, u, d].astype(F32)
            s1_ref[ch, u] = total.astype(BF16)
            for d in (2, 1, 3):
                copy2(ch, u, d).start()

    def start_3(ch):
        for u in range(UNITS):
            for d in range(1, 4):
                copy2(ch, u, d).wait_recv()
            here = along(axis_of(u, core), 1, 0)[0]
            total = s1_ref[ch, u, pl.ds(here * 4, 4)].astype(F32)
            for d in range(3):
                total = total + r2_ref[ch, u, d].astype(F32)
            s2_ref[ch, u] = total
            for d in (2, 1, 3):
                copy3(ch, u, d).start()

    def finish(ch):
        for u in range(UNITS):
            for d in range(1, 4):
                copy3(ch, u, d).wait_recv()
            here = along(axis_of(u, core), 2, 0)[0]
            total = s2_ref[ch, u, here]
            for d in range(3):
                total = total + r3_ref[ch, u, d]
            fin_ref[u] = total
        for cb in range(CB):
            out_ref[:, W * ch + 128 * cb : W * ch + 128 * cb + 128] = fin_ref[cb] / fin_ref[CB + cb]

    def compute(ch, between):
        filter_columns(0, ch, p_ref, h_ref, ya)

        def body(i, carry):
            g = 2 * i
            filter_columns((g + 1) * G, ch, p_ref, h_ref, yb)
            match_rows(g * G, ch, v_ref, ya, var_ref, kp_ref, sum_ref)
            filter_columns((g + 2) * G, ch, p_ref, h_ref, ya)
            match_rows((g + 1) * G, ch, v_ref, yb, var_ref, kp_ref, sum_ref)
            for turn, step in between:
                pl.when(i == turn)(step)
            return carry

        lax.fori_loop(0, NG // 2 - 1, body, 0)
        filter_columns((NG - 1) * G, ch, p_ref, h_ref, yb)
        match_rows((NG - 2) * G, ch, v_ref, ya, var_ref, kp_ref, sum_ref)
        match_rows((NG - 1) * G, ch, v_ref, yb, var_ref, kp_ref, sum_ref)

    for ch in range(NC):
        if ch == 0:
            compute(ch, ())
            pl.semaphore_wait(barrier, 10)
        else:
            last = ch - 1
            compute(ch, (
                (1, functools.partial(start_1, last)),
                (3, functools.partial(start_2, last)),
                (4, functools.partial(start_3, last)),
            ))
        start_core(ch)
        if ch > 0:
            finish(ch - 1)
    last = NC - 1
    start_1(last)
    start_2(last)
    start_3(last)
    finish(last)

    for ch in range(NC):
        for u in range(UNITS):
            core_copy(ch, u).wait_send()
            for d in range(1, 4):
                copy1(ch, u, d).wait_send()
                copy2(ch, u, d).wait_send()
                copy3(ch, u, d).wait_send()


def on_device(warp_image, warp_variance, kernel_coef, tile_patch):
    basis, horizontal, vertical = tables()
    images = jnp.transpose(warp_image, (1, 0, 2)).reshape(84 * T, COLS)
    vmem = pl.BlockSpec(memory_space=pltpu.VMEM)
    smem = pl.BlockSpec(memory_space=pltpu.SMEM)
    hbm = pl.BlockSpec(memory_space=pl.ANY)
    dma = pltpu.SemaphoreType.DMA
    out = pl.pallas_call(
        kernel,
        out_shape=jax.ShapeDtypeStruct((ROWS // 4, COLS), F32),
        in_specs=[hbm, hbm, vmem, smem, vmem, vmem, vmem],
        out_specs=vmem,
        scratch_shapes=[
            pltpu.VMEM((4, 84 * T, 128), F32),
            pltpu.VMEM((T, ROWS, COLS), F32),
            pltpu.VMEM((T, 4 * BLK, 256), BF16),
            pltpu.VMEM((T, ROWS, KDIM), BF16),
            pltpu.VMEM((T, KDIM), F32),
            pltpu.VMEM((G, KDIM, W), BF16),
            pltpu.VMEM((G, KDIM, W), BF16),
            pltpu.VMEM((T, 1, W), F32),
            pltpu.VMEM((2, T + 1, ROWS, W), F32),
            pltpu.VMEM((16, 128), jnp.int32),
            pltpu.SMEM((16, 128), jnp.int32),
            pltpu.VMEM((NC, UNITS, 64, 16, 128), BF16),
            pltpu.VMEM((UNITS, 64, 16, 128), F32),
            pltpu.VMEM((NC, UNITS, 64, 16, 128), BF16),
            pltpu.VMEM((NC, UNITS, 3, 16, 16, 128), BF16),
            pltpu.VMEM((NC, UNITS, 16, 16, 128), BF16),
            pltpu.VMEM((NC, UNITS, 3, 4, 16, 128), BF16),
            pltpu.VMEM((NC, UNITS, 4, 16, 128), F32),
            pltpu.VMEM((NC, UNITS, 3, 16, 128), F32),
            pltpu.VMEM((UNITS, 16, 128), F32),
            dma((24,)), dma((T,)), dma,
            dma((NC, UNITS)), dma((NC, UNITS)),
            dma((NC, UNITS, 3)), dma((NC, UNITS, 3)),
            dma((NC, UNITS, 3)), dma((NC, UNITS, 3)),
            dma((NC, UNITS, 3)), dma((NC, UNITS, 3)),
        ],
        compiler_params=pltpu.CompilerParams(
            collective_id=0, has_side_effects=True, vmem_limit_bytes=60 * 2**20),
        name="coadd",
    )(images, warp_variance, kernel_coef, tile_patch.reshape(1, T),
      jnp.asarray(basis), jnp.asarray(horizontal), jnp.asarray(vertical))
    return out[None]


def solution(mesh):
    return jax.shard_map(
        on_device,
        mesh=mesh,
        in_specs=(
            P(("visit", "patch"), None, None),
            P(("visit", "patch"), None, None),
            P(("visit", "patch"), None),
            P(("visit", "patch"), None),
        ),
        out_specs=P("patch", "visit", None),
        check_vma=False,
    )
```

time: 658 us -> 57.3 us (0.09); the launches traced: 650 us -> 56.5 us
  waiting for transfers between devices: 295 us -> 0 us
  other arithmetic: 136 us -> 0 us
  local copies, waits for them, and re-layouts: 101 us -> 1.38 us
  Pallas kernels: 0 us -> 55.2 us
  loops' own time: 49.5 us -> 0 us
  matrix products: 30.1 us -> 0 us
  starting transfers between devices: 25.2 us -> 0 us
  between operations: 13.6 us -> 0.01 us
    psum x1 -> x0, waiting for transfers between devices: 191 us -> none  [on_device(): numerator, denominator = lax.psum((numerator, denominator), 'visit')]
    all_to_all x3 -> x0, waiting for transfers between devices: 104 us -> none  [the longest x1 66.6 us: on_device(): lax.all_to_all(image_slots, 'patch', split_axis=0, concat_axis=0, tiled=T...]
    reduce_max x64 -> x0, other arithmetic: 98.9 us -> none  [match_slot(): jnp.max(slot_weight.astype(jnp.float32)) > 0.0]
    pallas_call x0 -> x1, Pallas kernels: none -> 55.2 us  [on_device(): pl.pallas_call(kernel, out_shape=jax.ShapeDtypeStruct((ROWS // 4, COLS),...]
    another operation x65 -> x0, loops' own time: 49.5 us -> none  [the longest x1 44.3 us: on_device(): matched = lax.map(match_slot, (got_image, got_kernel, got_weight))]
    dynamic_update_slice x64 -> x0, local copies, waits for them, and re-layouts: 40.2 us -> none  [on_device(): matched = lax.map(match_slot, (got_image, got_kernel, got_weight))]
    dot_general x41 -> x0, matrix products: 30.1 us -> none  [the longest x20 17.7 us: match_tile(): jnp.einsum('urjw,uwk->rjk', shifted, toeplitz, preferred_element_type=jnp...]
    convert_element_type x66 -> x0, other arithmetic: 27.3 us -> none  [the longest x64 22.4 us: band_table(): return (differ[None] == tap_ids).astype(jnp.bfloat16)]
  transfers between devices with their start and end apart: 4 -> 0, of which waited for: 3 -> 0; matrix products, arithmetic and copies ran while one was open for 4% -> 0% of each run, Pallas kernels for 0% -> 0%
where the time goes in v1:
time: 57.3 us; the launch traced here: 56.5 us
  Pallas kernels  55.2 us (96%)
  local copies, waits for them, and re-layouts  1.38 us (2%)
    pallas_call x1, Pallas kernels, on_device(): pl.pallas_call(kernel, out_shape=jax.ShapeDtypeStruct((ROWS // 4, COLS),...  55.2 us
    unnamed x1, local copies, waits for them, and re-layouts  1.38 us

profile of v1, /device:TPU:1, one launch (start us, length us, event | category | flops | bytes accessed | tf_op | source)
XLA Modules:
  0.0 56.5 jit_solution(1404340879589762237)
XLA Ops:
  0.0 55.2 %coadd.1 = f32[16,512]{1,0:T(8,128)} custom-call(f32[2016,512]{1,0:T(8,128)} %bitcast.5, f32[24,64,512]{2,1,0:T(8,128)} %var_hbm.1, f32[24,40]{1,0:T(8,128)} %c_ref.1, s32[1,24]{1,0:T(1,128)} %bitcast.7, f32[40,512]{1,0:T(8,128)} %constant.6.clone.bp_ref, bf16[256,1792]{1,0:T(8,128)(2,1)} %constant.7.clone.h_ref, f32[40,1280]{1,0:T(8,128)} %constant.8.clone.a_ref), custom_call_target="tpu_custom_call" | custom-call | tf_op jit(solution)/shard_map/coadd/pallas_call | solution.py:337
  55.2 1.4 %copy.9 = f32[1,16,512]{2,1,0:T(8,128)} copy(f32[1,16,512]{2,1,0:T(8,128)} %bitcast.6) | data formatting | bytes 65536

commit v2 on v1

--- a/solution.py
+++ b/solution.py
@@ -103,8 +103,8 @@
 def kernel(
     x_hbm, var_hbm, c_ref, tp_ref, bp_ref, h_ref, a_ref, out_ref,
     x_ref, var_ref, p_ref, v_ref, v0_ref, ya, yb, kp_ref, sum_ref,
-    iv_ref, idx_ref, d_ref, own_ref, rc_ref, r1_ref, s1_ref, r2_ref, s2_ref, r3_ref, fin_ref,
-    sx, sv, si, cs, cr, s1s, s1r, s2s, s2r, s3s, s3r,
+    iv_ref, idx_ref, d_ref, own_ref, rc_ref, r1_ref, s1_ref, r2_ref, fin_ref,
+    sx, sv, si, cs, cr, s1s, s1r, s2s, s2r,
 ):
     me_x = lax.axis_index("visit")
     me_p = lax.axis_index("patch")
@@ -136,6 +136,13 @@
             device(me_x, me_y, lax.rem(me_z + d, 4), core),
         ):
             pl.semaphore_signal(barrier, inc=1, device_id=who, device_id_type=MESH)
+        for e in range(1, 4):
+            for who in (
+                device(lax.rem(me_x + d, 4), lax.rem(me_y + e, 4), me_z, core),
+                device(me_x, lax.rem(me_y + d, 4), lax.rem(me_z + e, 4), core),
+                device(lax.rem(me_x + d, 4), me_y, lax.rem(me_z + e, 4), core),
+            ):
+                pl.semaphore_signal(barrier, inc=1, device_id=who, device_id_type=MESH)
 
     lane = lax.broadcasted_iota(jnp.int32, (8, 128), 1)
     one = jnp.full((8, 128), T, jnp.int32)
@@ -207,19 +214,22 @@
         here, there, who = along(axis_of(u, core), 0, d)
         return pltpu.make_async_remote_copy(
             src_ref=rc_ref.at[ch, u, pl.ds(there * 16, 16)], dst_ref=r1_ref.at[ch, u, d - 1],
-            send_sem=s1s.at[ch, u, d - 1], recv_sem=s1r.at[ch, u, d - 1], device_id=who, device_id_type=MESH)
+            send_sem=s1s.at[ch, u], recv_sem=s1r.at[ch, u], device_id=who, device_id_type=MESH)
 
     def copy2(ch, u, d):
-        here, there, who = along(axis_of(u, core), 1, d)
+        a = axis_of(u, core)
+        there2, who2 = along(a, 1, d // 4)[1:]
+        there3 = along(a, 2, d % 4)[1]
+        b2, b3 = lax.rem(a + 1, 3), lax.rem(a + 2, 3)
+        x = jnp.where(b2 == 0, there2, jnp.where(b3 == 0, there3, me_x))
+        y = jnp.where(b2 == 1, there2, jnp.where(b3 == 1, there3, me_y))
+        z = jnp.where(b2 == 2, there2, jnp.where(b3 == 2, there3, me_z))
         return pltpu.make_async_remote_copy(
-            src_ref=s1_ref.at[ch, u, pl.ds(there * 4, 4)], dst_ref=r2_ref.at[ch, u, d - 1],
-            send_sem=s2s.at[ch, u, d - 1], recv_sem=s2r.at[ch, u, d - 1], device_id=who, device_id_type=MESH)
-
-    def copy3(ch, u, d):
-        here, there, who = along(axis_of(u, core), 2, d)
-        return pltpu.make_async_remote_copy(
-            src_ref=s2_ref.at[ch, u, there], dst_ref=r3_ref.at[ch, u, d - 1],
-            send_sem=s3s.at[ch, u, d - 1], recv_sem=s3r.at[ch, u, d - 1], device_id=who, device_id_type=MESH)
+            src_ref=s1_ref.at[ch, u, there2 * 4 + there3], dst_ref=r2_ref.at[ch, u, d - 1],
+            send_sem=s2s.at[ch, u], recv_sem=s2r.at[ch, u], device_id=device(x, y, z, core), device_id_type=MESH)
+
+    def settle(ref, sem):
+        pltpu.make_async_copy(ref, ref, sem).wait()
 
     def start_core(ch):
         def put(u, place, value):
@@ -246,36 +256,22 @@
 
     def start_2(ch):
         for u in range(UNITS):
-            for d in range(1, 4):
-                copy1(ch, u, d).wait_recv()
+            settle(r1_ref.at[ch, u], s1r.at[ch, u])
             here = along(axis_of(u, core), 0, 0)[0]
             total = rc_ref[ch, u, pl.ds(here * 16, 16)].astype(F32)
             for d in range(3):
                 total = total + r1_ref[ch, u, d].astype(F32)
             s1_ref[ch, u] = total.astype(BF16)
-            for d in (2, 1, 3):
+            for d in range(1, 16):
                 copy2(ch, u, d).start()
 
-    def start_3(ch):
-        for u in range(UNITS):
-            for d in range(1, 4):
-                copy2(ch, u, d).wait_recv()
-            here = along(axis_of(u, core), 1, 0)[0]
-            total = s1_ref[ch, u, pl.ds(here * 4, 4)].astype(F32)
-            for d in range(3):
+    def finish(ch):
+        for u in range(UNITS):
+            settle(r2_ref.at[ch, u], s2r.at[ch, u])
+            a = axis_of(u, core)
+            total = s1_ref[ch, u, along(a, 1, 0)[0] * 4 + along(a, 2, 0)[0]].astype(F32)
+            for d in range(15):
                 total = total + r2_ref[ch, u, d].astype(F32)
-            s2_ref[ch, u] = total
-            for d in (2, 1, 3):
-                copy3(ch, u, d).start()
-
-    def finish(ch):
-        for u in range(UNITS):
-            for d in range(1, 4):
-                copy3(ch, u, d).wait_recv()
-            here = along(axis_of(u, core), 2, 0)[0]
-            total = s2_ref[ch, u, here]
-            for d in range(3):
-                total = total + r3_ref[ch, u, d]
             fin_ref[u] = total
         for cb in range(CB):
             out_ref[:, W * ch + 128 * cb : W * ch + 128 * cb + 128] = fin_ref[cb] / fin_ref[CB + cb]
@@ -298,33 +294,22 @@
         match_rows((NG - 2) * G, ch, v_ref, ya, var_ref, kp_ref, sum_ref)
         match_rows((NG - 1) * G, ch, v_ref, yb, var_ref, kp_ref, sum_ref)
 
+    compute(0, ())
+    pl.semaphore_wait(barrier, 37)
+    start_core(0)
+    compute(1, ((1, functools.partial(start_1, 0)),))
+    start_core(1)
+    start_2(0)
+    start_1(1)
+    finish(0)
+    start_2(1)
+    finish(1)
+
     for ch in range(NC):
-        if ch == 0:
-            compute(ch, ())
-            pl.semaphore_wait(barrier, 10)
-        else:
-            last = ch - 1
-            compute(ch, (
-                (1, functools.partial(start_1, last)),
-                (3, functools.partial(start_2, last)),
-                (4, functools.partial(start_3, last)),
-            ))
-        start_core(ch)
-        if ch > 0:
-            finish(ch - 1)
-    last = NC - 1
-    start_1(last)
-    start_2(last)
-    start_3(last)
-    finish(last)
-
-    for ch in range(NC):
         for u in range(UNITS):
             core_copy(ch, u).wait_send()
-            for d in range(1, 4):
-                copy1(ch, u, d).wait_send()
-                copy2(ch, u, d).wait_send()
-                copy3(ch, u, d).wait_send()
+            settle(r1_ref.at[ch, u], s1s.at[ch, u])
+            settle(r2_ref.at[ch, u], s2s.at[ch, u])
 
 
 def on_device(warp_image, warp_variance, kernel_coef, tile_patch):
@@ -356,15 +341,12 @@
             pltpu.VMEM((NC, UNITS, 64, 16, 128), BF16),
             pltpu.VMEM((NC, UNITS, 3, 16, 16, 128), BF16),
             pltpu.VMEM((NC, UNITS, 16, 16, 128), BF16),
-            pltpu.VMEM((NC, UNITS, 3, 4, 16, 128), BF16),
-            pltpu.VMEM((NC, UNITS, 4, 16, 128), F32),
-            pltpu.VMEM((NC, UNITS, 3, 16, 128), F32),
+            pltpu.VMEM((NC, UNITS, 15, 16, 128), BF16),
             pltpu.VMEM((UNITS, 16, 128), F32),
             dma((24,)), dma((T,)), dma,
             dma((NC, UNITS)), dma((NC, UNITS)),
-            dma((NC, UNITS, 3)), dma((NC, UNITS, 3)),
-            dma((NC, UNITS, 3)), dma((NC, UNITS, 3)),
-            dma((NC, UNITS, 3)), dma((NC, UNITS, 3)),
+            dma((NC, UNITS)), dma((NC, UNITS)),
+            dma((NC, UNITS)), dma((NC, UNITS)),
         ],
         compiler_params=pltpu.CompilerParams(
             collective_id=0, has_side_effects=True, vmem_limit_bytes=60 * 2**20),

time: 57.3 us -> 48.9 us (0.85); the launches traced: 56.5 us -> 48.7 us
  Pallas kernels: 55.2 us -> 47.4 us
    pallas_call x1, Pallas kernels: 55.2 us -> 47.4 us  [on_device(): pl.pallas_call(kernel, out_shape=jax.ShapeDtypeStruct((ROWS // 4, COLS),...]
where the time goes in v2:
time: 48.9 us; the launch traced here: 48.7 us
  Pallas kernels  47.4 us (97%)
  local copies, waits for them, and re-layouts  1.38 us (3%)
    pallas_call x1, Pallas kernels, on_device(): pl.pallas_call(kernel, out_shape=jax.ShapeDtypeStruct((ROWS // 4, COLS),...  47.4 us
    unnamed x1, local copies, waits for them, and re-layouts  1.38 us

profile of v2, /device:TPU:1, one launch (start us, length us, event | category | flops | bytes accessed | tf_op | source)
XLA Modules:
  0.0 48.7 jit_solution(17542858096236716806)
XLA Ops:
  0.0 47.4 %coadd.1 = f32[16,512]{1,0:T(8,128)} custom-call(f32[2016,512]{1,0:T(8,128)} %bitcast.5, f32[24,64,512]{2,1,0:T(8,128)} %var_hbm.1, f32[24,40]{1,0:T(8,128)} %c_ref.1, s32[1,24]{1,0:T(1,128)} %bitcast.7, f32[40,512]{1,0:T(8,128)} %constant.6.clone.bp_ref, bf16[256,1792]{1,0:T(8,128)(2,1)} %constant.7.clone.h_ref, f32[40,1280]{1,0:T(8,128)} %constant.8.clone.a_ref), custom_call_target="tpu_custom_call" | custom-call | tf_op jit(solution)/shard_map/coadd/pallas_call | solution.py:322
  47.4 1.4 %copy.9 = f32[1,16,512]{2,1,0:T(8,128)} copy(f32[1,16,512]{2,1,0:T(8,128)} %bitcast.6) | data formatting | bytes 65536

commit v3 on v2

v3 whole, which is shorter than its diff:
```python
import functools

import jax
import jax.numpy as jnp
import numpy as np
from jax import lax
from jax.experimental import pallas as pl
from jax.experimental.pallas import tpu as pltpu
from jax.sharding import PartitionSpec as P

KHALF = 10
TAPS = 2 * KHALF + 1
T = 24
ROWS = 64
COLS = 512
NPATCH = 32
BLK = 88
NK = 14
KDIM = 1280
CHUNKS = ((0, 2, 2), (2, 1, 4), (3, 1, 4))
PROWS = 368
PAT = (0, 88, 176, 272)
HI = lax.Precision.HIGHEST
F32 = jnp.float32
BF16 = jnp.bfloat16
MESH = pl.DeviceIdType.MESH


def tables():
    offsets = np.arange(TAPS, dtype=np.float64) - KHALF
    scaled = offsets / KHALF
    functions, place, terms = [], {}, []
    levels = ((1.0, 4), (2.5, 4), (5.0, 3))
    for s, (spread, degree) in enumerate(levels):
        profile = np.exp(-offsets * offsets / (2.0 * spread * spread))
        for i in range(degree + 1):
            place[s, i] = len(functions)
            functions.append(profile * scaled**i)
    for s, (spread, degree) in enumerate(levels):
        for i in range(degree + 1):
            for j in range(degree + 1 - i):
                terms.append((place[s, i], place[s, j]))
    g = np.array(functions)
    basis = np.zeros((len(terms), 512))
    for b, (ia, jb) in enumerate(terms):
        basis[b, : TAPS * TAPS] = np.outer(g[ia], g[jb]).reshape(-1)
    q = np.linalg.qr(g.T)[0]
    q = q.astype(jnp.bfloat16).astype(np.float64)
    mix = np.linalg.lstsq(q, g.T, rcond=None)[0]
    horizontal = np.zeros((256, NK * 128))
    for k in range(NK):
        for c in range(128):
            horizontal[c : c + TAPS, k * 128 + c] = q[:, k]
    vertical = np.zeros((len(terms), KDIM))
    for b, (ia, jb) in enumerate(terms):
        for k in range(NK):
            vertical[b, k * BLK : k * BLK + TAPS] = g[ia] * mix[k, jb]
    return basis.astype(np.float32), horizontal.astype(jnp.bfloat16), vertical.astype(np.float32)


def prepare_image(t, slot, x_ref, p_ref):
    x = jnp.concatenate([x_ref.at[j][pl.ds(t, 84, stride=T), :] for j in range(4)], axis=1)
    x = jnp.concatenate([x, jnp.zeros((BLK - 84, COLS), F32)], axis=0)
    x = jnp.concatenate([x, jnp.zeros((BLK, 128), F32)], axis=1)
    x = pltpu.roll(x, KHALF, 1)
    blocks = [x[:, 128 * j : 128 * j + 256] for j in range(4)]
    blocks.insert(3, jnp.zeros((8, 256), F32))
    blocks.append(jnp.zeros((8, 256), F32))
    p_ref[slot] = jnp.concatenate(blocks, axis=0).astype(BF16)


def prepare_band(t, slot, v_ref, v0_ref):
    row = jnp.broadcast_to(v0_ref[pl.ds(t, 1), :], (ROWS, KDIM))
    v_ref[slot] = pltpu.roll(row, 0, 1, stride=1, stride_axis=0).astype(BF16)


def filter_columns(first, group, block, cb, p_ref, h_ref, y_ref):
    rows = BLK * cb
    lhs = jnp.concatenate([p_ref[first + u, PAT[block] : PAT[block] + rows, :] for u in range(group)], axis=0)
    for m in range(NK // 2):
        r = jnp.dot(lhs, h_ref[:, 256 * m : 256 * m + 256], preferred_element_type=F32)
        for u in range(group):
            for b in range(cb):
                o = rows * u + BLK * b
                y = jnp.concatenate([r[o : o + BLK, :128], r[o : o + BLK, 128:]], axis=0)
                y_ref[u, 2 * BLK * m : 2 * BLK * m + 2 * BLK, 128 * b : 128 * b + 128] = y.astype(BF16)


def match_rows(tiles, first, group, block, cb, v_ref, y_ref, var_ref, kp_ref, sum_ref):
    cols = slice(128 * block, 128 * block + 128 * cb)
    for u in range(group):
        t = tiles + 4 * (u // 2) + u % 2
        matched = jnp.dot(v_ref[first + u], y_ref[u], preferred_element_type=F32)
        w = (1.0 / (var_ref[t, :, cols] * kp_ref[t][:, : 128 * cb])).astype(BF16).astype(F32)
        sum_ref[0, t, :, : 128 * cb] = w * matched
        sum_ref[1, t, :, : 128 * cb] = w


def place_coefs(a):
    cx = jnp.where(a == 0, 16, jnp.where(a == 1, 1, 4))
    cy = jnp.where(a == 0, 4, jnp.where(a == 1, 16, 1))
    cz = jnp.where(a == 0, 1, jnp.where(a == 1, 4, 16))
    return cx, cy, cz


def kernel(
    x_hbm, var_hbm, c_ref, tp_ref, bp_ref, h_hbm, a_ref, out_ref,
    x_ref, var_ref, h_ref, pe, po, ve, vo, v0_ref, ya2, yb2, ya1, yb1, kp_ref, sum_ref,
    iv_ref, idx_ref, own_ref, *rest,
):
    n = len(CHUNKS)
    m = n - 1
    dl_ref, ol_ref, rl_ref, el_ref = rest[5 * m : 5 * m + 4]
    sx, sv, si, sh, cs, cr, s1s, s1r, s2s, s2r, cls, clr, els, elr = rest[5 * m + 4 :]
    d_refs, rc_refs, r1_refs, s1_refs, r2_refs = (rest[i * m : i * m + m] for i in range(5))
    me_x = lax.axis_index("visit")
    me_p = lax.axis_index("patch")
    core = lax.rem(me_p, 2)
    me_y = lax.rem(me_p // 2, 4)
    me_z = me_p // 8

    def device(x, y, z, k):
        return (x, z * 8 + y * 2 + k)

    sibling = device(me_x, me_y, me_z, 1 - core)

    cpx = [
        pltpu.make_async_copy(
            x_hbm.at[pl.ds(T * 14 * (i // 4), T * 14), pl.ds(128 * (i % 4), 128)],
            x_ref.at[i % 4, pl.ds(T * 14 * (i // 4), T * 14)], sx.at[i])
        for i in range(24)
    ]
    cpv = [pltpu.make_async_copy(var_hbm.at[t], var_ref.at[t], sv.at[t]) for t in range(T)]
    cph = pltpu.make_async_copy(h_hbm, h_ref, sh)
    for cp in cpx + [cph] + cpv:
        cp.start()

    barrier = pltpu.get_barrier_semaphore()
    pl.semaphore_signal(barrier, inc=1, device_id=sibling, device_id_type=MESH)
    for d in range(1, 64):
        who = device(lax.rem(me_x + d // 4 % 4, 4), lax.rem(me_y + d % 4, 4), lax.rem(me_z + d // 16, 4), core)
        pl.semaphore_signal(barrier, inc=1, device_id=who, device_id_type=MESH)

    lane = lax.broadcasted_iota(jnp.int32, (8, 128), 1)
    one = jnp.full((8, 128), T, jnp.int32)
    two = one
    for t in range(T):
        hit = lane == tp_ref[0, t]
        two = jnp.where(hit, one, two)
        one = jnp.where(hit, t, one)
    iv_ref[0:8, :] = one
    iv_ref[8:16, :] = two
    cpi = pltpu.make_async_copy(iv_ref, idx_ref, si)
    cpi.start()

    c = c_ref[...]
    taps = jnp.dot(c, bp_ref[...], precision=HI, preferred_element_type=F32)
    kp = jnp.sum(taps * taps, axis=1, keepdims=True) / float(TAPS * TAPS) + 1e-6
    for t in range(T):
        kp_ref[t] = jnp.broadcast_to(kp[t : t + 1], (1, 256))
    v0_ref[...] = jnp.dot(c, a_ref[...], precision=HI, preferred_element_type=F32)
    for y in (ya2, yb2, ya1, yb1):
        for u in range(y.shape[0]):
            y[u, NK * BLK :, :] = jnp.zeros((KDIM - NK * BLK, y.shape[2]), BF16)
    for nd in range(2):
        sum_ref[nd, T] = jnp.zeros((ROWS, 256), F32)
    for cp in cpx:
        cp.wait()
    cph.wait()
    cpi.wait()

    def axis_of(ch, u, k):
        return lax.rem(u + k + ch, 3)

    def ring(b):
        here = jnp.where(b == 0, me_x, jnp.where(b == 1, me_y, me_z))
        to_v = jnp.where(b == 0, 1, 0)
        to_p = jnp.where(b == 0, 0, jnp.where(b == 1, 2, 8))
        places = [here] + [lax.rem(here + d, 4) for d in range(1, 4)]
        return [(at, (at - here) * to_v, (at - here) * to_p) for at in places]

    def units(ch):
        return CHUNKS[ch][1]

    def gather(ch, k, store):
        cbs = CHUNKS[ch][1]

        def body(i, carry):
            z, y = i // 4, lax.rem(i, 4)
            p = z * 8 + y * 2 + k
            i1, i2 = idx_ref[0, p], idx_ref[8, p]
            for nd in range(2):
                s = sum_ref[nd, i1, :, : 128 * cbs] + sum_ref[nd, i2, :, : 128 * cbs]
                for u in range(cbs):
                    cx, cy, cz = place_coefs(axis_of(ch, u, k))
                    for x in range(4):
                        store(u, cx * x + cy * y + cz * z, nd, s[16 * x : 16 * x + 16, 128 * u : 128 * u + 128])
            return carry
        lax.fori_loop(0, 16, body, 0)

    def core_copy(ch, u):
        return pltpu.make_async_remote_copy(
            src_ref=d_refs[ch].at[u], dst_ref=rc_refs[ch].at[u], send_sem=cs.at[ch, u], recv_sem=cr.at[ch, u],
            device_id=sibling, device_id_type=MESH)

    def settle(ref, sem):
        pltpu.make_async_copy(ref, ref, sem).wait()

    def start_core(ch):
        def put(u, place, nd, value):
            d_refs[ch][u, place, nd] = value.astype(BF16)
        gather(ch, 1 - core, put)
        for u in range(units(ch)):
            core_copy(ch, u).start()

        def keep(u, place, nd, value):
            own_ref[u, place, nd] = value
        gather(ch, core, keep)

    def start_1(ch):
        for u in range(units(ch)):
            core_copy(ch, u).wait_recv()
            around = ring(axis_of(ch, u, core))

            def body(i, carry):
                at = pl.ds(i * 4, 4)
                rc_refs[ch][u, at] = (rc_refs[ch][u, at].astype(F32) + own_ref[u, at]).astype(BF16)
                return carry
            lax.fori_loop(0, 16, body, 0)
            for d in (2, 1, 3):
                there, v, p = around[d]
                pltpu.make_async_remote_copy(
                    src_ref=rc_refs[ch].at[u, pl.ds(there * 16, 16)], dst_ref=r1_refs[ch].at[u, d - 1],
                    send_sem=s1s.at[ch, u], recv_sem=s1r.at[ch, u],
                    device_id=(me_x + v, me_p + p), device_id_type=MESH).start()

    def start_2(ch):
        for u in range(units(ch)):
            a = axis_of(ch, u, core)
            here = ring(a)[0][0]
            second, third = ring(lax.rem(a + 1, 3)), ring(lax.rem(a + 2, 3))
            settle(r1_refs[ch].at[u], s1r.at[ch, u])
            total = rc_refs[ch][u, pl.ds(here * 16, 16)].astype(F32)
            for d in range(3):
                total = total + r1_refs[ch][u, d].astype(F32)
            s1_refs[ch][u] = total.astype(BF16)
            for d in (10, 6, 9, 11, 14, 2, 8, 5, 7, 13, 15, 1, 3, 4, 12):
                at2, v2, p2 = second[d // 4]
                at3, v3, p3 = third[d % 4]
                pltpu.make_async_remote_copy(
                    src_ref=s1_refs[ch].at[u, at2 * 4 + at3], dst_ref=r2_refs[ch].at[u, d - 1],
                    send_sem=s2s.at[ch, u], recv_sem=s2r.at[ch, u],
                    device_id=(me_x + v2 + v3, me_p + p2 + p3), device_id_type=MESH).start()

    def finish(ch):
        for u in range(units(ch)):
            a = axis_of(ch, u, core)
            here = ring(lax.rem(a + 1, 3))[0][0] * 4 + ring(lax.rem(a + 2, 3))[0][0]
            settle(r2_refs[ch].at[u], s2r.at[ch, u])
            total = s1_refs[ch][u, here].astype(F32)
            for d in range(15):
                total = total + r2_refs[ch][u, d].astype(F32)
            at = 128 * (CHUNKS[ch][0] + u)
            out_ref[:, at : at + 128] = total[0] / total[1]

    def last_gather(dz, k, store):
        z = lax.rem(me_z + dz, 4)

        def body(y, carry):
            p = z * 8 + y * 2 + k
            i1, i2 = idx_ref[0, p], idx_ref[8, p]
            for nd in range(2):
                s = sum_ref[nd, i1, :, :128] + sum_ref[nd, i2, :, :128]
                for x in range(4):
                    store(dz, x * 4 + y, nd, s[16 * x : 16 * x + 16])
            return carry
        lax.fori_loop(0, 4, body, 0)

    def last_copy(dz):
        return pltpu.make_async_remote_copy(
            src_ref=dl_ref.at[dz], dst_ref=rl_ref.at[dz], send_sem=cls.at[dz], recv_sem=clr.at[dz],
            device_id=sibling, device_id_type=MESH)

    def last_core():
        def put(dz, place, nd, value):
            dl_ref[dz, place, nd] = value.astype(BF16)

        def keep(dz, place, nd, value):
            ol_ref[dz, place, nd] = value
        for dz in (2, 1, 3, 0):
            last_gather(dz, 1 - core, put)
            last_copy(dz).start()
        for dz in (2, 1, 3, 0):
            last_gather(dz, core, keep)

    def last_spread():
        for dz in (2, 1, 3, 0):
            last_copy(dz).wait_recv()
            rl_ref[dz] = (rl_ref[dz].astype(F32) + ol_ref[dz]).astype(BF16)
            z = lax.rem(me_z + dz, 4)
            for dx in (2, 1, 3, 0):
                x = lax.rem(me_x + dx, 4)
                for dy in (2, 1, 3, 0):
                    y = lax.rem(me_y + dy, 4)
                    slot = dz * 16 + dx * 4 + dy - 1
                    if slot >= 0:
                        pltpu.make_async_remote_copy(
                            src_ref=rl_ref.at[dz, x * 4 + y], dst_ref=el_ref.at[slot], send_sem=els, recv_sem=elr,
                            device_id=device(x, y, z, core), device_id_type=MESH).start()

    def last_finish():
        settle(el_ref, elr)
        total = rl_ref[0, me_x * 4 + me_y].astype(F32)

        def body(i, total):
            for k in range(9):
                total = total + el_ref[i * 9 + k].astype(F32)
            return total
        total = lax.fori_loop(0, 7, body, total)
        out_ref[:, COLS - 128 :] = total[0] / total[1]

    def compute(ch, between):
        block, cb, group = CHUNKS[ch]
        ya, yb = (ya2, yb2) if cb == 2 else (ya1, yb1)
        ng = T // group

        def images(g, parity):
            for u in range(group):
                t = 2 * g * group + 2 * parity + u
                prepare_image(t, g * group + u, x_ref, (pe, po)[parity])

        def bands(g, parity):
            for u in range(group):
                t = 2 * g * group + 2 * parity + u
                prepare_band(t, g * group + u, (ve, vo)[parity], v0_ref)

        def where(g, parity):
            return (pe, po)[parity], (ve, vo)[parity], g * group, 2 * g * group + 2 * parity

        def filters(g, parity, y):
            p, v, slot, t = where(g, parity)
            filter_columns(slot, group, block, cb, p, h_ref, y)

        def matches(g, parity, y):
            p, v, slot, t = where(g, parity)
            match_rows(t, slot, group, block, cb, v, y, var_ref, kp_ref, sum_ref)

        if ch == 0:
            for g, parity in ((0, 0), (0, 1), (1, 0)):
                images(g, parity)
                bands(g, parity)
            for cp in cpv:
                cp.wait()
        filters(0, 0, ya)

        def body(i, carry):
            after = jnp.minimum(i + 2, ng // 2 - 1)
            filters(i, 1, yb)
            if ch == 0:
                images(i + 1, 1)
            matches(i, 0, ya)
            if ch == 0:
                bands(after, 0)
            filters(i + 1, 0, ya)
            if ch == 0:
                images(after, 0)
            matches(i, 1, yb)
            if ch == 0:
                bands(i + 1, 1)
            for turn, step in between:
                pl.when(i == turn)(step)
            return carry

        lax.fori_loop(0, ng // 2 - 1, body, 0)
        filters(ng // 2 - 1, 1, yb)
        matches(ng // 2 - 1, 0, ya)
        matches(ng // 2 - 1, 1, yb)

    compute(0, ())
    pl.semaphore_wait(barrier, 64)
    start_core(0)
    compute(1, ((0, functools.partial(start_1, 0)),))
    start_core(1)
    compute(2, ((0, functools.partial(start_1, 1)),))
    last_core()
    start_2(0)
    last_spread()
    start_2(1)
    finish(0)
    finish(1)
    last_finish()

    for dz in range(4):
        last_copy(dz).wait_send()
    settle(el_ref, els)
    for ch in range(n - 1):
        for u in range(units(ch)):
            core_copy(ch, u).wait_send()
            settle(r1_refs[ch].at[u], s1s.at[ch, u])
            settle(r2_refs[ch].at[u], s2s.at[ch, u])


def on_device(warp_image, warp_variance, kernel_coef, tile_patch):
    basis, horizontal, vertical = tables()
    images = jnp.transpose(warp_image, (1, 0, 2)).reshape(84 * T, COLS)
    vmem = pl.BlockSpec(memory_space=pltpu.VMEM)
    smem = pl.BlockSpec(memory_space=pltpu.SMEM)
    hbm = pl.BlockSpec(memory_space=pl.ANY)
    dma = pltpu.SemaphoreType.DMA
    units = [chunk[1] for chunk in CHUNKS[:-1]]
    out = pl.pallas_call(
        kernel,
        out_shape=jax.ShapeDtypeStruct((ROWS // 4, COLS), F32),
        in_specs=[hbm, hbm, vmem, smem, vmem, hbm, vmem],
        out_specs=vmem,
        scratch_shapes=[
            pltpu.VMEM((4, 84 * T, 128), F32),
            pltpu.VMEM((T, ROWS, COLS), F32),
            pltpu.VMEM((256, NK * 128), BF16),
            pltpu.VMEM((T // 2, PROWS, 256), BF16),
            pltpu.VMEM((T // 2, PROWS, 256), BF16),
            pltpu.VMEM((T // 2, ROWS, KDIM), BF16),
            pltpu.VMEM((T // 2, ROWS, KDIM), BF16),
            pltpu.VMEM((T, KDIM), F32),
            pltpu.VMEM((2, KDIM, 256), BF16),
            pltpu.VMEM((2, KDIM, 256), BF16),
            pltpu.VMEM((4, KDIM, 128), BF16),
            pltpu.VMEM((4, KDIM, 128), BF16),
            pltpu.VMEM((T, 1, 256), F32),
            pltpu.VMEM((2, T + 1, ROWS, 256), F32),
            pltpu.VMEM((16, 128), jnp.int32),
            pltpu.SMEM((16, 128), jnp.int32),
            pltpu.VMEM((2, 64, 2, 16, 128), F32),
            *[pltpu.VMEM((u, 64, 2, 16, 128), BF16) for u in units],
            *[pltpu.VMEM((u, 64, 2, 16, 128), BF16) for u in units],
            *[pltpu.VMEM((u, 3, 16, 2, 16, 128), BF16) for u in units],
            *[pltpu.VMEM((u, 16, 2, 16, 128), BF16) for u in units],
            *[pltpu.VMEM((u, 15, 2, 16, 128), BF16) for u in units],
            pltpu.VMEM((4, 16, 2, 16, 128), BF16),
            pltpu.VMEM((4, 16, 2, 16, 128), F32),
            pltpu.VMEM((4, 16, 2, 16, 128), BF16),
            pltpu.VMEM((63, 2, 16, 128), BF16),
            dma((24,)), dma((T,)), dma, dma,
            *[dma((len(units), 2))] * 6,
            dma((4,)), dma((4,)), dma, dma,
        ],
        compiler_params=pltpu.CompilerParams(
            collective_id=0, has_side_effects=True, vmem_limit_bytes=60 * 2**20),
        name="coadd",
    )(images, warp_variance, kernel_coef, tile_patch.reshape(1, T),
      jnp.asarray(basis), jnp.asarray(horizontal), jnp.asarray(vertical))
    return out[None]


def solution(mesh):
    return jax.shard_map(
        on_device,
        mesh=mesh,
        in_specs=(
            P(("visit", "patch"), None, None),
            P(("visit", "patch"), None, None),
            P(("visit", "patch"), None),
            P(("visit", "patch"), None),
        ),
        out_specs=P("patch", "visit", None),
        check_vma=False,
    )
```

time: 48.9 us -> 44.5 us (0.910)
  the two profiles are of different devices: /device:TPU:1 before, /device:TPU:0 now
where the time goes in v3:
time: 44.5 us; the launch traced here: 44.3 us
  Pallas kernels  42.9 us (96%)
  local copies, waits for them, and re-layouts  1.38 us (3%)
    pallas_call x1, Pallas kernels, on_device(): pl.pallas_call(kernel, out_shape=jax.ShapeDtypeStruct((ROWS // 4, COLS),...  42.9 us
    unnamed x1, local copies, waits for them, and re-layouts  1.38 us

profile of v3, /device:TPU:0, one launch (start us, length us, event | category | flops | bytes accessed | tf_op | source)
XLA Modules:
  0.0 44.3 jit_solution(12307942214912501438)
XLA Ops:
  0.0 42.9 %coadd.1 = f32[16,512]{1,0:T(8,128)} custom-call(f32[2016,512]{1,0:T(8,128)} %bitcast.5, f32[24,64,512]{2,1,0:T(8,128)} %var_hbm.1, f32[24,40]{1,0:T(8,128)} %c_ref.1, s32[1,24]{1,0:T(1,128)} %bitcast.7, f32[40,512]{1,0:T(8,128)} %constant.6.clone.bp_ref, bf16[256,1792]{1,0:T(8,128)(2,1)} %constant.7.clone.h_hbm, f32[40,1280]{1,0:T(8,128)} %constant.8.clone.a_ref), custom_call_target="tpu_custom_call" | custom-call | tf_op jit(solution)/shard_map/coadd/pallas_call | solution.py:411
  42.9 1.4 %copy.9 = f32[1,16,512]{2,1,0:T(8,128)} copy(f32[1,16,512]{2,1,0:T(8,128)} %bitcast.6) | data formatting | bytes 65536

commit v4 on v3

--- a/solution.py
+++ b/solution.py
@@ -170,7 +170,7 @@
     cpi.wait()
 
     def axis_of(ch, u, k):
-        return lax.rem(u + k + ch, 3)
+        return lax.rem(u + k + ch * k, 3)
 
     def ring(b):
         here = jnp.where(b == 0, me_x, jnp.where(b == 1, me_y, me_z))
@@ -196,7 +196,7 @@
                     for x in range(4):
                         store(u, cx * x + cy * y + cz * z, nd, s[16 * x : 16 * x + 16, 128 * u : 128 * u + 128])
             return carry
-        lax.fori_loop(0, 16, body, 0)
+        lax.fori_loop(0, 16, body, 0, unroll=4)
 
     def core_copy(ch, u):
         return pltpu.make_async_remote_copy(
@@ -217,8 +217,8 @@
             own_ref[u, place, nd] = value
         gather(ch, core, keep)
 
-    def start_1(ch):
-        for u in range(units(ch)):
+    def start_1(ch, some=None):
+        for u in some or range(units(ch)):
             core_copy(ch, u).wait_recv()
             around = ring(axis_of(ch, u, core))
 
@@ -274,7 +274,7 @@
                 for x in range(4):
                     store(dz, x * 4 + y, nd, s[16 * x : 16 * x + 16])
             return carry
-        lax.fori_loop(0, 4, body, 0)
+        lax.fori_loop(0, 4, body, 0, unroll=4)
 
     def last_copy(dz):
         return pltpu.make_async_remote_copy(
@@ -379,12 +379,12 @@
     compute(0, ())
     pl.semaphore_wait(barrier, 64)
     start_core(0)
-    compute(1, ((0, functools.partial(start_1, 0)),))
+    compute(1, ((0, functools.partial(start_1, 0, (0,))), (1, functools.partial(start_1, 0, (1,)))))
     start_core(1)
     compute(2, ((0, functools.partial(start_1, 1)),))
     last_core()
+    last_spread()
     start_2(0)
-    last_spread()
     start_2(1)
     finish(0)
     finish(1)

time: 44.5 us -> 42.6 us (0.957)
  the two profiles are of different devices: /device:TPU:0 before, /device:TPU:1 now
where the time goes in v4:
time: 42.6 us; the launch traced here: 42.4 us
  Pallas kernels  41 us (96%)
  local copies, waits for them, and re-layouts  1.38 us (3%)
    pallas_call x1, Pallas kernels, on_device(): pl.pallas_call(kernel, out_shape=jax.ShapeDtypeStruct((ROWS // 4, COLS),...  41 us
    unnamed x1, local copies, waits for them, and re-layouts  1.38 us

profile of v4, /device:TPU:1, one launch (start us, length us, event | category | flops | bytes accessed | tf_op | source)
XLA Modules:
  0.0 42.4 jit_solution(3120314367559313504)
XLA Ops:
  0.0 41.0 %coadd.1 = f32[16,512]{1,0:T(8,128)} custom-call(f32[2016,512]{1,0:T(8,128)} %bitcast.5, f32[24,64,512]{2,1,0:T(8,128)} %var_hbm.1, f32[24,40]{1,0:T(8,128)} %c_ref.1, s32[1,24]{1,0:T(1,128)} %bitcast.7, f32[40,512]{1,0:T(8,128)} %constant.6.clone.bp_ref, bf16[256,1792]{1,0:T(8,128)(2,1)} %constant.7.clone.h_hbm, f32[40,1280]{1,0:T(8,128)} %constant.8.clone.a_ref), custom_call_target="tpu_custom_call" | custom-call | tf_op jit(solution)/shard_map/coadd/pallas_call | solution.py:411
  41.0 1.4 %copy.9 = f32[1,16,512]{2,1,0:T(8,128)} copy(f32[1,16,512]{2,1,0:T(8,128)} %bitcast.6) | data formatting | bytes 65536

commit v5 on v4

--- a/solution.py
+++ b/solution.py
@@ -359,6 +359,9 @@
             if ch == 0:
                 images(i + 1, 1)
             matches(i, 0, ya)
+            for turn, step in between:
+                if turn < 0:
+                    pl.when(i == 0)(step)
             if ch == 0:
                 bands(after, 0)
             filters(i + 1, 0, ya)
@@ -368,7 +371,8 @@
             if ch == 0:
                 bands(i + 1, 1)
             for turn, step in between:
-                pl.when(i == turn)(step)
+                if turn >= 0:
+                    pl.when(i == turn)(step)
             return carry
 
         lax.fori_loop(0, ng // 2 - 1, body, 0)
@@ -381,7 +385,7 @@
     start_core(0)
     compute(1, ((0, functools.partial(start_1, 0, (0,))), (1, functools.partial(start_1, 0, (1,)))))
     start_core(1)
-    compute(2, ((0, functools.partial(start_1, 1)),))
+    compute(2, ((-1, functools.partial(start_1, 1)),))
     last_core()
     last_spread()
     start_2(0)

time: 42.6 us -> 42.8 us (level)
  no operation moved by 1% of the time
where the time goes in v5:
time: 42.8 us; the launch traced here: 42.6 us
  Pallas kernels  41.2 us (96%)
  local copies, waits for them, and re-layouts  1.38 us (3%)
    pallas_call x1, Pallas kernels, on_device(): pl.pallas_call(kernel, out_shape=jax.ShapeDtypeStruct((ROWS // 4, COLS),...  41.2 us
    unnamed x1, local copies, waits for them, and re-layouts  1.38 us

profile of v5, /device:TPU:1, one launch (start us, length us, event | category | flops | bytes accessed | tf_op | source)
XLA Modules:
  0.0 42.6 jit_solution(15843273101227263233)
XLA Ops:
  0.0 41.2 %coadd.1 = f32[16,512]{1,0:T(8,128)} custom-call(f32[2016,512]{1,0:T(8,128)} %bitcast.5, f32[24,64,512]{2,1,0:T(8,128)} %var_hbm.1, f32[24,40]{1,0:T(8,128)} %c_ref.1, s32[1,24]{1,0:T(1,128)} %bitcast.7, f32[40,512]{1,0:T(8,128)} %constant.6.clone.bp_ref, bf16[256,1792]{1,0:T(8,128)(2,1)} %constant.7.clone.h_hbm, f32[40,1280]{1,0:T(8,128)} %constant.8.clone.a_ref), custom_call_target="tpu_custom_call" | custom-call | tf_op jit(solution)/shard_map/coadd/pallas_call | solution.py:415
  41.2 1.4 %copy.9 = f32[1,16,512]{2,1,0:T(8,128)} copy(f32[1,16,512]{2,1,0:T(8,128)} %bitcast.6) | data formatting | bytes 65536
